TPU v7x, 512 devices: a whole 4x4x16 slice. The times are simulated.
512 devices in a mesh: seq: 16 (over z_lo, y), dp: 32 (over x, z_hi, core).
Axes of the slice: x: 4, y: 4, z: 16 (z_hi: 4, z_lo: 4; z = z_hi * 4 + z_lo), core: 2. Of those that a mesh axis runs over, the one named last changes fastest.
Arguments:
- frames: bfloat16 [32, 3072, 1536], P('dp', 'seq'), may hold values from -6 to 6
- queries: bfloat16 [32, 3072, 1536], P('dp', 'seq'), may hold values from -16 to 16
- keys: bfloat16 [32, 3072, 1536], P('dp', 'seq'), may hold values from -16 to 16
- values: bfloat16 [32, 3072, 1536], P('dp', 'seq'), may hold values from -24 to 24
- lengths: int32 [32], P('dp'), may hold values from 1536 to 3072, as said below
- out_proj: bfloat16 [1536, 1536], P(None, 'dp'), may hold values from -0.15625 to 0.15625
- conv_kernel: float32 [31, 1536], replicated, may hold values from -1 to 1
- cotangent: bfloat16 [32, 3072, 1536], P('dp', 'seq'), may hold values from -6 to 6
Outputs:
- block_out: bfloat16 [32, 3072, 1536], P('dp', 'seq')
- grad_hidden: bfloat16 [32, 3072, 1536], P('dp', 'seq')
- grad_context: bfloat16 [32, 3072, 1536], P('dp', 'seq')
- grad_kernel: float32 [31, 1536], replicated
Inputs may be any that keep to these rules, and one draw needn't show every extreme that they name: `lengths`: one utterance has 3072 valid frames and another 3072 // 2.
All inputs are finite; a program needn't handle non-finite values.
Results may differ from a plain program's by a relative error of at most 0.0062.
Values may be sent and summed in bfloat16 or wider, within the bound.
No kernel may reach another device: no remote copies, remote signals or barrier semaphores. Data moves between devices by JAX's collectives and lax.ppermute only.
A program may use at most 64 MiB of HBM per device.

v0:
```python
import math
import jax
import jax.numpy as jnp
from jax import lax
from jax.sharding import PartitionSpec as P

KERNEL = 31
HEAD_DIM = 96


def with_halo(block, sides, width):
    for axis, dim in sides:
        count = lax.axis_size(axis)
        forward = [(i, i + 1) for i in range(count - 1)]
        backward = [(target, source) for source, target in forward]
        low = lax.ppermute(
            lax.slice_in_dim(block, block.shape[dim] - width, None, axis=dim), axis, forward
        )
        high = lax.ppermute(lax.slice_in_dim(block, 0, width, axis=dim), axis, backward)
        block = jnp.concatenate([low, block, high], axis=dim)
    return block


def attend_heads(query_heads, key_heads, value_heads, key_valid):
    total_frames = query_heads.shape[0]
    head_count = query_heads.shape[1]
    block_rows = math.gcd(total_frames, 1024)
    blocks = query_heads.reshape(total_frames // block_rows, block_rows, head_count, HEAD_DIM)
    softmax_scale = HEAD_DIM ** (-0.5)

    def one_block(query_block):
        scores = (
            jnp.einsum("qhe,khe->hqk", query_block, key_heads, preferred_element_type=jnp.float32)
            * softmax_scale
        )
        scores = jnp.where(key_valid[None, None, :], scores, -jnp.inf)
        largest = jnp.max(scores, axis=-1, keepdims=True)
        expd = jnp.exp(scores - largest)
        weights = (expd / jnp.sum(expd, axis=-1, keepdims=True)).astype(jnp.bfloat16)
        return jnp.einsum(
            "hqk,khe->qhe", weights, value_heads, preferred_element_type=jnp.float32
        ).astype(jnp.bfloat16)

    return lax.map(one_block, blocks).reshape(total_frames, head_count * HEAD_DIM)


def local(frames, queries, keys, values, lengths, out_proj, conv_kernel, cotangent):
    frames_dev = frames.shape[1]
    groups = lax.axis_size("seq")
    length_all = frames_dev * groups
    half_width = KERNEL // 2
    first_frame = lax.axis_index("seq") * frames_dev
    valid_local = first_frame + jnp.arange(frames_dev, dtype=jnp.int32) < lengths[0]
    key_valid = jnp.arange(length_all, dtype=jnp.int32) < lengths[0]
    query_group, key_group, value_group = (
        lax.all_to_all(queries, "seq", split_axis=2, concat_axis=1, tiled=True),
        lax.all_to_all(keys, "seq", split_axis=2, concat_axis=1, tiled=True),
        lax.all_to_all(values, "seq", split_axis=2, concat_axis=1, tiled=True),
    )
    head_count = query_group.shape[2] // HEAD_DIM
    context_heads = attend_heads(
        query_group[0].reshape(length_all, head_count, HEAD_DIM),
        key_group[0].reshape(length_all, head_count, HEAD_DIM),
        value_group[0].reshape(length_all, head_count, HEAD_DIM),
        key_valid,
    )
    context = lax.all_to_all(context_heads[None], "seq", split_axis=1, concat_axis=2, tiled=True)[0]
    mixed = jnp.dot(
        context,
        lax.all_gather(out_proj, "dp", axis=1, tiled=True),
        preferred_element_type=jnp.float32,
    )
    hidden = (frames[0].astype(jnp.float32) + mixed).astype(jnp.bfloat16)
    conv_input = jnp.where(valid_local[:, None], hidden, jnp.zeros((), jnp.bfloat16))
    padded = with_halo(conv_input[None], (("seq", 1),), half_width)[0]
    conv = jnp.zeros((frames_dev, conv_input.shape[1]), jnp.float32)
    for offset in range(KERNEL):
        conv = conv + conv_kernel[offset] * padded[offset : offset + frames_dev].astype(jnp.float32)
    sigma = jax.nn.sigmoid(conv)
    block_out = (hidden.astype(jnp.float32) + conv * sigma).astype(jnp.bfloat16)
    grad_out = cotangent[0].astype(jnp.float32)
    conv_grad = (grad_out * sigma * (1.0 + conv * (1.0 - sigma))).astype(jnp.bfloat16)
    grad_float = conv_grad.astype(jnp.float32)
    kernel_terms = []
    for offset in range(KERNEL):
        kernel_terms.append(
            jnp.sum(grad_float * padded[offset : offset + frames_dev].astype(jnp.float32), axis=0)
        )
    total_count = length_all * lax.axis_size("dp")
    grad_kernel = lax.psum(jnp.stack(kernel_terms), ("seq", "dp")) / math.sqrt(total_count)
    grad_padded = with_halo(conv_grad[None], (("seq", 1),), half_width)[0]
    back = jnp.zeros((frames_dev, conv_input.shape[1]), jnp.float32)
    for offset in range(KERNEL):
        begin = 2 * half_width - offset
        back = back + conv_kernel[offset] * grad_padded[begin : begin + frames_dev].astype(
            jnp.float32
        )
    grad_hidden = (grad_out + jnp.where(valid_local[:, None], back, 0.0)).astype(jnp.bfloat16)
    grad_context = lax.dot_general(
        grad_hidden,
        lax.all_gather(out_proj, "dp", axis=1, tiled=True),
        (((1,), (1,)), ((), ())),
        preferred_element_type=jnp.float32,
    )
    grad_context = grad_context.astype(jnp.bfloat16)
    return (block_out[None], grad_hidden[None], grad_context[None], grad_kernel)


def solution(mesh):
    in_specs = (
        P("dp", "seq", None),
        P("dp", "seq", None),
        P("dp", "seq", None),
        P("dp", "seq", None),
        P("dp"),
        P(None, "dp"),
        P(),
        P("dp", "seq", None),
    )
    out_specs = (P("dp", "seq", None), P("dp", "seq", None), P("dp", "seq", None), P())
    return jax.shard_map(local, mesh=mesh, in_specs=in_specs, out_specs=out_specs, check_vma=False)
```

profile of v0, /device:TPU:1, one launch (start us, length us, event | category | flops | bytes accessed | tf_op | source)
XLA Modules:
  0.0 701.6 jit_solution(153183562824020149)
XLA Ops:
  7.2 3.5 copy.31
  11.2 8.8 %reduce.66 = bf16[1536,192]{1,0:T(8,128)(2,1)S(1)} reduce(bf16[1536,1,192]{2,1,0:T(2,128)(2,1)S(1)} %bitcast.821, bf16[]{:T(256)} %broadcast.335), dimensions={1}, to_apply=%bitcast.766.reduce_sub_computation | reduce | bytes 1179650
  21.8 9.2 %all-to-all-start = ((bf16[16,2,9216]{2,1,0:T(2,128)(2,1)}), bf16[16,2,9216]{2,1,0:T(2,128)(2,1)S(1)}, u32[]{:S(2)}, u32[]{:S(2)}) async-start(bf16[16,2,9216]{2,1,0:T(2,128)(2,1)} %reshape.719), calls=%async_computation | async-start | bytes 1179648 | tf_op jit(solution)/shard_map/all_to_all | solution.py:56
  32.2 8.8 %reduce.67 = bf16[1536,192]{1,0:T(8,128)(2,1)S(1)} reduce(bf16[1536,1,192]{2,1,0:T(2,128)(2,1)S(1)} %bitcast.823, bf16[]{:T(256)} %broadcast.335), dimensions={1}, to_apply=%bitcast.768.reduce_sub_computation | reduce | bytes 1179650
  45.5 5.7 all-to-all-start.1
  52.5 8.8 %reduce.68 = bf16[1536,192]{1,0:T(8,128)(2,1)S(1)} reduce(bf16[1536,1,192]{2,1,0:T(2,128)(2,1)S(1)} %bitcast.824, bf16[]{:T(256)} %broadcast.335), dimensions={1}, to_apply=%bitcast.770.reduce_sub_computation | reduce | bytes 1179650
  65.2 6.1 all-to-all-start.2
  80.2 5.1 all-to-all-done.2
  85.3 4.8 reshape.724
  94.0 28.7 %while.11 = (s32[]{:T(128)}, bf16[3,1024,1,96]{1,3,2,0:T(8,128)(2,1)S(1)}, bf16[3,1024,1,96]{1,3,2,0:T(8,128)(2,1)S(1)}, bf16[3072,1,96]{0,2,1:T(8,128)(2,1)S(1)...) while((s32[]{:T(128)}, bf16[3,1024,1,96]{1,3,2,0:T(8,128)(2,1)S(1)}, ...), condition=%wide.region_3.4_spmd.clone, body=%wide.region_0.3_spmd.clone.sunk | while | flops 1245807616 | bytes 39354456 | solution.py:44
  99.6 4.0 fusion.346
  109.1 4.0 fusion.346
  118.6 4.0 fusion.346
  123.4 17.3 %reduce.69 = bf16[3072,96]{1,0:T(8,128)(2,1)S(1)} reduce(bf16[3072,1,96]{2,1,0:T(2,128)(2,1)S(1)} %bitcast.822, bf16[]{:T(256)} %broadcast.335), dimensions={1}, to_apply=%bitcast.772.reduce_sub_computation | reduce | bytes 1179650
  142.8 6.0 all-to-all-start.3
  149.9 35.1 %all-to-all-done.3 = bf16[16,2,9216]{2,1,0:T(2,128)(2,1)S(1)} async-done(((bf16[16,2,9216]{2,1,0:T(2,128)(2,1)}), bf16[16,2,9216]{2,1,0:T(2,128)(2,1)S(1)}, u32[]{:S(2)}, u32[]{:S(2)}) %all-to-all-start.3) | async-done | bytes 589856 | tf_op jit(solution)/shard_map/all_to_all | solution.py:67
  190.8 4.0 fusion.16
  198.6 3.9 collective-permute-done.1
  202.5 6.0 fusion.208
  209.8 4.0 collective-permute-start.3
  213.8 7.3 %fusion.239 = (f32[1536]{0:T(1024)S(1)}, f32[1536]{0:T(1024)S(1)}, f32[1536]{0:T(1024)S(1)}, f32[1536]{0:T(1024)S(1)}, f32[1536]{0:T(1024)S(1)}, /*index=5*/f32[...) fusion(bf16[1,15,1536]{2,1,0:T(8,128)(2,1)S(1)} %collective-permute-done.1, ...), kind=kLoop, calls=%fused_computation.457 | loop fusion | flops 67820544 | bytes 3858624 | tf_op jit(solution)/shard_map/reduce_sum | solution.py:87
  230.7 6.5 fusion.209
  237.2 8.9 %fusion.17 = bf16[1,192,1536]{2,1,0:T(8,128)(2,1)} fusion(bf16[1536,1536]{0,1:T(8,128)(2,1)} %all-gather.2.cloned.1.call-done, bf16[1,192,1536]{2,1,0:T(8,128)(2,1)S(1)} %copy-done, bf16[1,192,1536]{2,1,0:T(8,128)(2,1)S(1)} %fusion.208, bf16[1,15,1536]{2,1,0:T(8,128)(2,1)S(1)} %collective-permute-done.3, ...), kind=kOutput, calls=%fused_computation.109 | convolution fusion | flops 961118208 | bytes 6770880 | tf_op jit(solution)/shard_map/dot_general | solution.py:99
  246.2 446.7 %all-reduce.2.cloned.1.call-done = f32[31,1536]{1,0:T(8,128)} async-done(((f32[31,1536]{1,0:T(8,128)}), f32[31,1536]{1,0:T(8,128)}) %all-reduce.2.cloned.1.call-update) | async-done | bytes 190480 | tf_op jit(solution)/shard_map/psum | solution.py:90
  (107 shorter events, 66.7 us)
Async XLA Ops:
  20.0 10.9 %copy-start.1 = (bf16[1,192,1536]{2,1,0:T(8,128)(2,1)S(1)}, bf16[1,192,1536]{2,1,0:T(8,128)(2,1)}, u32[]{:S(2)}) copy-start(bf16[1,192,1536]{2,1,0:T(8,128)(2,1)} %param.12) | copy-start | bytes 1769476
  21.8 23.8 %all-to-all-start = ((bf16[16,2,9216]{2,1,0:T(2,128)(2,1)}), bf16[16,2,9216]{2,1,0:T(2,128)(2,1)S(1)}, u32[]{:S(2)}, u32[]{:S(2)}) async-start(bf16[16,2,9216]{2,1,0:T(2,128)(2,1)} %reshape.719), calls=%async_computation | async-start | bytes 1179648 | tf_op jit(solution)/shard_map/all_to_all | solution.py:56
  42.7 8.5 %copy-start.2 = (bf16[1,192,1536]{2,1,0:T(8,128)(2,1)S(1)}, bf16[1,192,1536]{2,1,0:T(8,128)(2,1)}, u32[]{:S(2)}) copy-start(bf16[1,192,1536]{2,1,0:T(8,128)(2,1)} %param.13) | copy-start | bytes 1769476
  45.5 19.7 %all-to-all-start.1 = ((bf16[16,2,9216]{2,1,0:T(2,128)(2,1)}), bf16[16,2,9216]{2,1,0:T(2,128)(2,1)S(1)}, u32[]{:S(2)}, u32[]{:S(2)}) async-start(bf16[16,2,9216]{2,1,0:T(2,128)(2,1)} %reshape.721), calls=%async_computation.1 | async-start | bytes 1179648 | tf_op jit(solution)/shard_map/all_to_all | solution.py:57
  65.2 20.1 %all-to-all-start.2 = ((bf16[16,2,9216]{2,1,0:T(2,128)(2,1)}), bf16[16,2,9216]{2,1,0:T(2,128)(2,1)}, u32[]{:S(2)}, u32[]{:S(2)}) async-start(bf16[16,2,9216]{2,1,0:T(2,128)(2,1)} %reshape.723), calls=%async_computation.2 | async-start | bytes 1179648 | tf_op jit(solution)/shard_map/all_to_all | solution.py:58
  71.4 119.4 %all-gather.2.cloned.1.call-start = ((), (), s32[]{:S(2)}) async-start(), calls=%async_computation.4 | async-start | bytes 4866048 | tf_op jit(solution)/shard_map/all_gather | solution.py:70
  91.8 2.2 copy-start.3
  140.8 8.8 %copy-start.4 = (f32[31,1536]{1,0:T(8,128)S(1)}, f32[31,1536]{1,0:T(8,128)}, u32[]{:S(2)}) copy-start(f32[31,1536]{1,0:T(8,128)} %param.16) | copy-start | bytes 571396
  142.8 42.2 %all-to-all-start.3 = ((bf16[16,2,9216]{2,1,0:T(2,128)(2,1)}), bf16[16,2,9216]{2,1,0:T(2,128)(2,1)S(1)}, u32[]{:S(2)}, u32[]{:S(2)}) async-start(bf16[16,2,9216]{2,1,0:T(2,128)(2,1)} %reshape.725), calls=%async_computation.3 | async-start | bytes 1179648 | tf_op jit(solution)/shard_map/all_to_all | solution.py:67
  148.8 544.1 %all-reduce.2.cloned.1.call-start = ((), (), s32[]{:S(2)}) async-start(), calls=%async_computation.5 | async-start | bytes 393216 | tf_op jit(solution)/shard_map/psum | solution.py:90
  188.6 2.2 copy-start.5
  194.8 7.7 %copy-start = (bf16[1,192,1536]{2,1,0:T(8,128)(2,1)S(1)}, bf16[1,192,1536]{2,1,0:T(8,128)(2,1)}, u32[]{:S(2)}) copy-start(bf16[1,192,1536]{2,1,0:T(8,128)(2,1)} %param.17) | copy-start | bytes 1769476
  194.9 3.6 collective-permute-start
  197.1 5.4 collective-permute-start.1
  208.5 22.2 %collective-permute-start.2 = (bf16[1,15,1536]{2,1,0:T(8,128)(2,1)S(1)}, bf16[1,15,1536]{2,1,0:T(8,128)(2,1)S(1)}, u32[]{:S(2)}, u32[]{:S(2)}) collective-permute-start(bf16[1,15,1536]{2,1,0:T(8,128)(2,1)S(1)} %get-tuple-element.152), channel_id=1, source_target_pairs={{32,0},{64,32},{96,64},{128,96},{160,128},{192,160},{224,192},{256... | collective-permute-start | bytes 138248 | tf_op jit(solution)/shard_map/ppermute | solution.py:19
  209.8 20.9 %collective-permute-start.3 = (bf16[1,15,1536]{2,1,0:T(8,128)(2,1)S(1)}, bf16[1,15,1536]{2,1,0:T(8,128)(2,1)S(1)}, u32[]{:S(2)}, u32[]{:S(2)}) collective-permute-start(bf16[1,15,1536]{2,1,0:T(8,128)(2,1)S(1)} %get-tuple-element.153), channel_id=1, source_target_pairs={{0,32},{32,64},{64,96},{96,128},{128,160},{160,192},{192,224},{224... | collective-permute-start | bytes 138248 | tf_op jit(solution)/shard_map/ppermute | solution.py:16
Sparse Core Ops, SparseCore 0:
  75.3 107.3 all-gather.1
  230.8 462.0 all-reduce.1
where the time goes:
time: 711 us; the launch traced here: 702 us
  waiting for transfers between devices  496 us (70%)
  other arithmetic  81.8 us (12%)
  local copies, waits for them, and re-layouts  40.2 us (6%)
  starting transfers between devices  36 us (5%)
  matrix products  31.2 us (4%)
  between operations  15.7 us (2%)
    psum x1, waiting for transfers between devices, local(): lax.psum(jnp.stack(kernel_terms), ('seq', 'dp')) / math.sqrt(total_count)  447 us
    unnamed x4, other arithmetic  43.9 us
    all_to_all x1, waiting for transfers between devices, local(): lax.all_to_all(context_heads[None], 'seq', split_axis=1, concat_axis=2, t...  35.1 us
    unnamed x25, local copies, waits for them, and re-layouts  22.1 us
  transfers between devices with their start and end apart: 10, of which 6 were waited for; matrix products, arithmetic and copies ran while one was open for 18% of the time, Pallas kernels for 0%

commit v1 on v0

--- a/solution.py
+++ b/solution.py
@@ -87,7 +87,7 @@
             jnp.sum(grad_float * padded[offset : offset + frames_dev].astype(jnp.float32), axis=0)
         )
     total_count = length_all * lax.axis_size("dp")
-    grad_kernel = lax.psum(jnp.stack(kernel_terms), ("seq", "dp")) / math.sqrt(total_count)
+    grad_kernel = lax.psum(lax.psum(jnp.stack(kernel_terms), "seq"), "dp") / math.sqrt(total_count)
     grad_padded = with_halo(conv_grad[None], (("seq", 1),), half_width)[0]
     back = jnp.zeros((frames_dev, conv_input.shape[1]), jnp.float32)
     for offset in range(KERNEL):

time: 711 us -> 750 us (1.055)
  waiting for transfers between devices: 496 us -> 536 us
    psum x1 -> x2, waiting for transfers between devices: 447 us -> 486 us  [the longest x1 332 us: local(): lax.psum(lax.psum(jnp.stack(kernel_terms), 'seq'), 'dp')]
  transfers between devices with their start and end apart: 10 -> 11, of which waited for: 6 -> 7; matrix products, arithmetic and copies ran while one was open for 18% -> 17% of each run, Pallas kernels for 0% -> 0%
where the time goes in v1:
time: 750 us; the launch traced here: 741 us
  waiting for transfers between devices  536 us (71%)
  other arithmetic  82 us (11%)
  local copies, waits for them, and re-layouts  40.2 us (5%)
  starting transfers between devices  36.2 us (5%)
  matrix products  31.2 us (4%)
  between operations  15.3 us (2%)
    psum x1, waiting for transfers between devices, local(): lax.psum(lax.psum(jnp.stack(kernel_terms), 'seq'), 'dp')  332 us
    psum x1, waiting for transfers between devices, local(): lax.psum(jnp.stack(kernel_terms), 'seq')  154 us
    unnamed x4, other arithmetic  43.7 us
    all_to_all x1, waiting for transfers between devices, local(): lax.all_to_all(context_heads[None], 'seq', split_axis=1, concat_axis=2, t...  35 us
    unnamed x25, local copies, waits for them, and re-layouts  22.1 us
  transfers between devices with their start and end apart: 11, of which 7 were waited for; matrix products, arithmetic and copies ran while one was open for 17% of the time, Pallas kernels for 0%

profile of v1, /device:TPU:1, one launch (start us, length us, event | category | flops | bytes accessed | tf_op | source)
XLA Modules:
  0.0 741.2 jit_solution(10455947053107178280)
XLA Ops:
  11.2 8.8 %reduce.66 = bf16[1536,192]{1,0:T(8,128)(2,1)S(1)} reduce(bf16[1536,1,192]{2,1,0:T(2,128)(2,1)S(1)} %bitcast.821, bf16[]{:T(256)} %broadcast.335), dimensions={1}, to_apply=%bitcast.766.reduce_sub_computation | reduce | bytes 1179650
  21.8 9.2 %all-to-all-start = ((bf16[16,2,9216]{2,1,0:T(2,128)(2,1)}), bf16[16,2,9216]{2,1,0:T(2,128)(2,1)S(1)}, u32[]{:S(2)}, u32[]{:S(2)}) async-start(bf16[16,2,9216]{2,1,0:T(2,128)(2,1)} %reshape.719), calls=%async_computation | async-start | bytes 1179648 | tf_op jit(solution)/shard_map/all_to_all | solution.py:56
  32.2 8.8 %reduce.67 = bf16[1536,192]{1,0:T(8,128)(2,1)S(1)} reduce(bf16[1536,1,192]{2,1,0:T(2,128)(2,1)S(1)} %bitcast.823, bf16[]{:T(256)} %broadcast.335), dimensions={1}, to_apply=%bitcast.768.reduce_sub_computation | reduce | bytes 1179650
  45.5 5.7 all-to-all-start.1
  52.5 8.8 %reduce.68 = bf16[1536,192]{1,0:T(8,128)(2,1)S(1)} reduce(bf16[1536,1,192]{2,1,0:T(2,128)(2,1)S(1)} %bitcast.824, bf16[]{:T(256)} %broadcast.335), dimensions={1}, to_apply=%bitcast.770.reduce_sub_computation | reduce | bytes 1179650
  65.2 6.1 all-to-all-start.2
  80.2 5.1 all-to-all-done.2
  85.3 4.8 reshape.724
  94.0 28.7 %while.11 = (s32[]{:T(128)}, bf16[3,1024,1,96]{1,3,2,0:T(8,128)(2,1)S(1)}, bf16[3,1024,1,96]{1,3,2,0:T(8,128)(2,1)S(1)}, bf16[3072,1,96]{0,2,1:T(8,128)(2,1)S(1)...) while((s32[]{:T(128)}, bf16[3,1024,1,96]{1,3,2,0:T(8,128)(2,1)S(1)}, ...), condition=%wide.region_3.4_spmd.clone, body=%wide.region_0.3_spmd.clone.sunk | while | flops 1245807616 | bytes 39354456 | solution.py:44
  99.6 4.0 fusion.346
  109.1 4.0 fusion.346
  118.6 4.0 fusion.346
  123.4 17.2 %reduce.69 = bf16[3072,96]{1,0:T(8,128)(2,1)S(1)} reduce(bf16[3072,1,96]{2,1,0:T(2,128)(2,1)S(1)} %bitcast.822, bf16[]{:T(256)} %broadcast.335), dimensions={1}, to_apply=%bitcast.772.reduce_sub_computation | reduce | bytes 1179650
  142.7 6.0 all-to-all-start.3
  149.7 35.0 %all-to-all-done.3 = bf16[16,2,9216]{2,1,0:T(2,128)(2,1)S(1)} async-done(((bf16[16,2,9216]{2,1,0:T(2,128)(2,1)}), bf16[16,2,9216]{2,1,0:T(2,128)(2,1)S(1)}, u32[]{:S(2)}, u32[]{:S(2)}) %all-to-all-start.3) | async-done | bytes 589856 | tf_op jit(solution)/shard_map/all_to_all | solution.py:67
  190.5 4.0 fusion.16
  198.5 3.9 collective-permute-done.1
  202.4 6.0 fusion.208
  209.7 4.0 collective-permute-start.3
  213.7 7.6 %fusion.239 = (f32[1536]{0:T(1024)S(1)}, f32[1536]{0:T(1024)S(1)}, f32[1536]{0:T(1024)S(1)}, f32[1536]{0:T(1024)S(1)}, f32[1536]{0:T(1024)S(1)}, /*index=5*/f32[...) fusion(bf16[1,15,1536]{2,1,0:T(8,128)(2,1)S(1)} %collective-permute-done.1, ...), kind=kLoop, calls=%fused_computation.457 | loop fusion | flops 67820544 | bytes 3858624 | tf_op jit(solution)/shard_map/reduce_sum | solution.py:87
  231.0 6.5 fusion.209
  237.5 154.4 %all-reduce.3.cloned.1.call-done = f32[31,1536]{1,0:T(8,128)} async-done(((f32[31,1536]{1,0:T(8,128)}), f32[31,1536]{1,0:T(8,128)}) %all-reduce.3.cloned.1.call-update) | async-done | bytes 190480 | tf_op jit(solution)/shard_map/psum | solution.py:90
  391.9 8.9 %fusion.17 = bf16[1,192,1536]{2,1,0:T(8,128)(2,1)} fusion(bf16[1536,1536]{0,1:T(8,128)(2,1)} %all-gather.2.cloned.1.call-done, bf16[1,192,1536]{2,1,0:T(8,128)(2,1)S(1)} %copy-done, bf16[1,192,1536]{2,1,0:T(8,128)(2,1)S(1)} %fusion.208, bf16[1,15,1536]{2,1,0:T(8,128)(2,1)S(1)} %collective-permute-done.3, ...), kind=kOutput, calls=%fused_computation.109 | convolution fusion | flops 961118208 | bytes 6770880 | tf_op jit(solution)/shard_map/dot_general | solution.py:99
  400.9 332.0 %all-reduce.5.cloned.1.call-done = f32[31,1536]{1,0:T(8,128)} async-done(((f32[31,1536]{1,0:T(8,128)}), f32[31,1536]{1,0:T(8,128)}) %all-reduce.5.cloned.1.call-update) | async-done | bytes 190480 | tf_op jit(solution)/shard_map/psum | solution.py:90
  (110 shorter events, 70.5 us)
Async XLA Ops:
  20.0 10.9 %copy-start.1 = (bf16[1,192,1536]{2,1,0:T(8,128)(2,1)S(1)}, bf16[1,192,1536]{2,1,0:T(8,128)(2,1)}, u32[]{:S(2)}) copy-start(bf16[1,192,1536]{2,1,0:T(8,128)(2,1)} %param.12) | copy-start | bytes 1769476
  21.8 23.8 %all-to-all-start = ((bf16[16,2,9216]{2,1,0:T(2,128)(2,1)}), bf16[16,2,9216]{2,1,0:T(2,128)(2,1)S(1)}, u32[]{:S(2)}, u32[]{:S(2)}) async-start(bf16[16,2,9216]{2,1,0:T(2,128)(2,1)} %reshape.719), calls=%async_computation | async-start | bytes 1179648 | tf_op jit(solution)/shard_map/all_to_all | solution.py:56
  42.7 8.5 %copy-start.2 = (bf16[1,192,1536]{2,1,0:T(8,128)(2,1)S(1)}, bf16[1,192,1536]{2,1,0:T(8,128)(2,1)}, u32[]{:S(2)}) copy-start(bf16[1,192,1536]{2,1,0:T(8,128)(2,1)} %param.13) | copy-start | bytes 1769476
  45.5 19.7 %all-to-all-start.1 = ((bf16[16,2,9216]{2,1,0:T(2,128)(2,1)}), bf16[16,2,9216]{2,1,0:T(2,128)(2,1)S(1)}, u32[]{:S(2)}, u32[]{:S(2)}) async-start(bf16[16,2,9216]{2,1,0:T(2,128)(2,1)} %reshape.721), calls=%async_computation.1 | async-start | bytes 1179648 | tf_op jit(solution)/shard_map/all_to_all | solution.py:57
  65.2 20.1 %all-to-all-start.2 = ((bf16[16,2,9216]{2,1,0:T(2,128)(2,1)}), bf16[16,2,9216]{2,1,0:T(2,128)(2,1)}, u32[]{:S(2)}, u32[]{:S(2)}) async-start(bf16[16,2,9216]{2,1,0:T(2,128)(2,1)} %reshape.723), calls=%async_computation.2 | async-start | bytes 1179648 | tf_op jit(solution)/shard_map/all_to_all | solution.py:58
  71.4 119.1 %all-gather.2.cloned.1.call-start = ((), (), s32[]{:S(2)}) async-start(), calls=%async_computation.4 | async-start | bytes 4866048 | tf_op jit(solution)/shard_map/all_gather | solution.py:70
  91.8 2.2 copy-start.3
  140.6 8.8 %copy-start.4 = (f32[31,1536]{1,0:T(8,128)S(1)}, f32[31,1536]{1,0:T(8,128)}, u32[]{:S(2)}) copy-start(f32[31,1536]{1,0:T(8,128)} %param.16) | copy-start | bytes 571396
  142.7 42.0 %all-to-all-start.3 = ((bf16[16,2,9216]{2,1,0:T(2,128)(2,1)}), bf16[16,2,9216]{2,1,0:T(2,128)(2,1)S(1)}, u32[]{:S(2)}, u32[]{:S(2)}) async-start(bf16[16,2,9216]{2,1,0:T(2,128)(2,1)} %reshape.725), calls=%async_computation.3 | async-start | bytes 1179648 | tf_op jit(solution)/shard_map/all_to_all | solution.py:67
  148.7 243.2 %all-reduce.3.cloned.1.call-start = ((), (), s32[]{:S(2)}) async-start(), calls=%async_computation.5 | async-start | bytes 393216 | tf_op jit(solution)/shard_map/psum | solution.py:90
  188.3 2.2 copy-start.5
  194.5 7.9 %copy-start = (bf16[1,192,1536]{2,1,0:T(8,128)(2,1)S(1)}, bf16[1,192,1536]{2,1,0:T(8,128)(2,1)}, u32[]{:S(2)}) copy-start(bf16[1,192,1536]{2,1,0:T(8,128)(2,1)} %param.17) | copy-start | bytes 1769476
  194.7 3.9 collective-permute-start
  197.0 5.4 collective-permute-start.1
  208.4 22.6 %collective-permute-start.2 = (bf16[1,15,1536]{2,1,0:T(8,128)(2,1)S(1)}, bf16[1,15,1536]{2,1,0:T(8,128)(2,1)S(1)}, u32[]{:S(2)}, u32[]{:S(2)}) collective-permute-start(bf16[1,15,1536]{2,1,0:T(8,128)(2,1)S(1)} %get-tuple-element.152), channel_id=1, source_target_pairs={{32,0},{64,32},{96,64},{128,96},{160,128},{192,160},{224,192},{256... | collective-permute-start | bytes 138248 | tf_op jit(solution)/shard_map/ppermute | solution.py:19
  209.7 21.3 %collective-permute-start.3 = (bf16[1,15,1536]{2,1,0:T(8,128)(2,1)S(1)}, bf16[1,15,1536]{2,1,0:T(8,128)(2,1)S(1)}, u32[]{:S(2)}, u32[]{:S(2)}) collective-permute-start(bf16[1,15,1536]{2,1,0:T(8,128)(2,1)S(1)} %get-tuple-element.153), channel_id=1, source_target_pairs={{0,32},{32,64},{64,96},{96,128},{128,160},{160,192},{192,224},{224... | collective-permute-start | bytes 138248 | tf_op jit(solution)/shard_map/ppermute | solution.py:16
  231.0 501.9 %all-reduce.5.cloned.1.call-start = ((), (), s32[]{:S(2)}) async-start(), calls=%async_computation.6 | async-start | bytes 393216 | tf_op jit(solution)/shard_map/psum | solution.py:90
Sparse Core Ops, SparseCore 0:
  75.3 107.3 all-gather.1
  231.1 160.7 all-reduce.2
  395.1 337.7 all-reduce.4
